TPU v7x, 512 devices: a whole 4x4x16 slice. The times are simulated.
512 devices in a mesh: dom: 64 (over x, z), sub: 8 (over y, core).
Axes of the slice: x: 4, y: 4, z: 16, core: 2. Of those that a mesh axis runs over, the one named last changes fastest.
Arguments:
- right_side: float32 [1024, 16, 128], P(('dom', 'sub')), as said below
- diag_blocks: float32 [1024, 128, 128], P(('dom', 'sub')), as said below
- block_values: float32 [1024, 4, 128, 128], P(('dom', 'sub')), as said below
- block_cols: int32 [1024, 4], P(('dom', 'sub')), may hold values from 0 to 31, as said below
- block_count: int32 [1024], P(('dom', 'sub')), may hold values from 0 to 4, as said below
- cell_diagonal: float32 [1024, 128], P(('dom', 'sub')), as said below
Outputs:
- solution_field: float32 [1024, 16, 128], P(('dom', 'sub'))
- residual: float32 [1024, 16, 128], P(('dom', 'sub'))
Inputs may be any that keep to these rules, and one draw needn't show every extreme that they name: `block_cols`: live slots of a block row point to distinct block rows that come after it in the window (positions 0 to 15 are the block rows of the same index of dom, the rest those of the next index); block rows of the last index of dom point only into their own index; dead slots hold 0. `block_count`: the number of live slots, which varies from device to device. `block_values`: entries lie between -1 / 128 and 0. `diag_blocks`: entries lie between -1 / 128 and 0. `cell_diagonal`: every entry exceeds 1 + the live slots of its block row + the live slots of all block rows that couple to its block row, so the operator is strictly diagonally dominant. `right_side`: entries lie between -50 and 50.
All inputs are finite; a program needn't handle non-finite values.
Results may differ from a plain program's by a relative error of at most 0.00065.
Values sent between devices are 32-bit elements; how exact they have to be, the bound alone decides.
A program may use at most 64 MiB of HBM per device.

v0:
```python
import jax
import jax.numpy as jnp
from jax import lax
from jax.sharding import PartitionSpec as P

K = 4
ITERS = 3
PRECISE = lax.Precision.HIGHEST


def passed_along(x, axis, by):
    peers = lax.axis_size(axis)
    pairs = [(i, i + by) for i in range(peers) if 0 <= i + by < peers]
    return lax.ppermute(x, axis, pairs)


def local(right_side, diag_blocks, block_values, block_cols, block_count, cell_diagonal):
    rows_dev = right_side.shape[0]
    group_rows = lax.axis_size("sub") * rows_dev
    upper_part = jnp.triu(diag_blocks, 1)
    live_slots = jnp.arange(K, dtype=jnp.int32)[None, :] < block_count[:, None]
    window_ids = jnp.arange(2 * group_rows, dtype=jnp.int32)
    picker = (
        (block_cols[:, :, None] == window_ids[None, None, :]) & live_slots[:, :, None]
    ).astype(jnp.float32)

    def local_dots(first, second):
        return jnp.sum(first * second, axis=(0, 2))

    def residual_sum(residual_now, precond_now):
        return lax.psum(local_dots(residual_now, precond_now), ("dom", "sub"))

    solution_field = jnp.zeros_like(right_side)
    residual = right_side
    precond_res = residual / cell_diagonal[:, None, :]
    direction = precond_res
    precond_dot = residual_sum(residual, precond_res)
    for iteration in range(ITERS):
        own_part = jnp.einsum("rab,rzb->rza", upper_part, direction, precision=PRECISE)
        own_part = own_part + jnp.einsum("rba,rzb->rza", upper_part, direction, precision=PRECISE)
        own_part = own_part + cell_diagonal[:, None, :] * direction
        own_group = lax.all_gather(direction, "sub", axis=0, tiled=True)
        next_group = passed_along(own_group, "dom", -1)
        window = jnp.concatenate([own_group, next_group], axis=0)
        far_rows = jnp.einsum("rkw,wzb->rkzb", picker, window, precision=PRECISE)
        forward = jnp.einsum("rkab,rkzb->rza", block_values, far_rows, precision=PRECISE)
        back_terms = jnp.einsum("rkba,rzb->rkza", block_values, direction, precision=PRECISE)
        spread = jnp.einsum("rkw,rkza->wza", picker, back_terms, precision=PRECISE)
        incoming = passed_along(spread[group_rows:], "dom", 1)
        back_own = lax.psum_scatter(
            spread[:group_rows] + incoming, "sub", scatter_dimension=0, tiled=True
        )
        image_vec = own_part + forward + back_own
        curvature = lax.psum(local_dots(direction, image_vec), ("dom", "sub"))
        step_size = precond_dot / curvature
        solution_field = solution_field + step_size[None, :, None] * direction
        residual = residual - step_size[None, :, None] * image_vec
        if iteration + 1 < ITERS:
            precond_res = residual / cell_diagonal[:, None, :]
            new_dot = residual_sum(residual, precond_res)
            direction = precond_res + (new_dot / precond_dot)[None, :, None] * direction
            precond_dot = new_dot
    return (solution_field, residual)


def solution(mesh):
    return jax.shard_map(
        local,
        mesh=mesh,
        in_specs=(
            P(("dom", "sub"), None, None),
            P(("dom", "sub"), None, None),
            P(("dom", "sub"), None, None, None),
            P(("dom", "sub"), None),
            P(("dom", "sub")),
            P(("dom", "sub"), None),
        ),
        out_specs=(P(("dom", "sub"), None, None), P(("dom", "sub"), None, None)),
        check_vma=False,
    )
```

profile of v0, /device:TPU:1, one launch (start us, length us, event | category | flops | bytes accessed | tf_op | source)
XLA Modules:
  0.0 715.4 jit_solution(11586665640421009732)
XLA Ops:
  7.2 0.8 broadcast_divide_fusion
  8.0 19.6 %all_gather.9 = f32[16,16,128]{2,1,0:T(8,128)S(1)} all-gather(f32[2,16,128]{2,1,0:T(8,128)S(1)} %broadcast_divide_fusion), channel_id=1, replica_groups=mesh['dom'=64,'sub'=8] {'sub'}, dimensions={0}, use_global_device_ids=true | all-gather | bytes 147456 | tf_op jit(solution)/shard_map/all_gather | solution.py:42
  27.6 1.4 collective-permute-start
  30.3 4.0 collective-permute-start.1
  35.0 1.7 collective-permute-done.1
  36.7 0.7 copy_add_fusion.2
  37.5 0.5 convolution_bitcast_fusion.5
  38.2 37.2 %reduce-scatter.4.cloned.1.call-done = f32[2,16,128]{2,1,0:T(8,128)} async-done(((f32[16,16,128]{2,1,0:T(8,128)}), f32[2,16,128]{2,1,0:T(8,128)}) %reduce-scatter.4.cloned.1.call-update) | async-done | bytes 16400 | tf_op jit(solution)/shard_map/reduce_scatter | solution.py:50
  75.4 0.8 multiply_reduce_fusion.4
  76.2 105.7 %all-reduce = (f32[16]{0:T(128)S(1)}, f32[16]{0:T(128)S(1)}) all-reduce(f32[16]{0:T(128)S(1)} %get-tuple-element.3, f32[16]{0:T(128)S(1)} %get-tuple-element.2), channel_id=1, replica_groups=mesh['dom'=64,'sub'=8] {'dom','sub'}, use_global_device_ids=true, to_apply=%region_1.2 | all-reduce | flops 32 | bytes 256 | tf_op jit(solution)/shard_map/psum | solution.py:31
  182.2 99.4 %psum.44 = f32[16]{0:T(128)S(1)} all-reduce(f32[16]{0:T(128)S(1)} %get-tuple-element.12), channel_id=1, replica_groups=mesh['dom'=64,'sub'=8] {'dom','sub'}, use_global_device_ids=true, to_apply=%region_6.7 | all-reduce | flops 16 | bytes 128 | tf_op jit(solution)/shard_map/psum | solution.py:31
  281.7 13.2 %all_gather.10 = f32[16,16,128]{2,1,0:T(8,128)S(1)} all-gather(f32[2,16,128]{2,1,0:T(8,128)S(1)} %multiply_add_fusion.2), channel_id=1, replica_groups=mesh['dom'=64,'sub'=8] {'sub'}, dimensions={0}, use_global_device_ids=true | all-gather | bytes 147456 | tf_op jit(solution)/shard_map/all_gather | solution.py:42
  295.3 1.3 collective-permute-start.2
  297.1 4.0 collective-permute-start.3
  301.3 0.7 collective-permute-done.2
  302.4 1.0 collective-permute-done.3
  303.4 0.7 copy_add_fusion.1
  304.2 0.5 convolution_bitcast_fusion.4
  305.0 33.6 %reduce-scatter.6.cloned.1.call-done = f32[2,16,128]{2,1,0:T(8,128)} async-done(((f32[16,16,128]{2,1,0:T(8,128)}), f32[2,16,128]{2,1,0:T(8,128)}) %reduce-scatter.6.cloned.1.call-update) | async-done | bytes 16400 | tf_op jit(solution)/shard_map/reduce_scatter | solution.py:50
  338.5 0.8 multiply_reduce_fusion.2
  339.4 105.7 %psum.45 = f32[16]{0:T(128)S(1)} all-reduce(f32[16]{0:T(128)S(1)} %get-tuple-element.10), channel_id=1, replica_groups=mesh['dom'=64,'sub'=8] {'dom','sub'}, use_global_device_ids=true, to_apply=%region_9.10 | all-reduce | flops 16 | bytes 128 | tf_op jit(solution)/shard_map/psum | solution.py:54
  445.3 99.2 %psum.46 = f32[16]{0:T(128)S(1)} all-reduce(f32[16]{0:T(128)S(1)} %get-tuple-element.8), channel_id=1, replica_groups=mesh['dom'=64,'sub'=8] {'dom','sub'}, use_global_device_ids=true, to_apply=%region_11.12 | all-reduce | flops 16 | bytes 128 | tf_op jit(solution)/shard_map/psum | solution.py:31
  544.6 13.2 %all_gather.11 = f32[16,16,128]{2,1,0:T(8,128)S(1)} all-gather(f32[2,16,128]{2,1,0:T(8,128)S(1)} %multiply_add_fusion.1), channel_id=1, replica_groups=mesh['dom'=64,'sub'=8] {'sub'}, dimensions={0}, use_global_device_ids=true | all-gather | bytes 147456 | tf_op jit(solution)/shard_map/all_gather | solution.py:42
  558.2 1.3 collective-permute-start.4
  560.0 4.0 collective-permute-start.5
  564.2 0.7 collective-permute-done.4
  565.3 1.0 collective-permute-done.5
  566.3 0.7 copy_add_fusion
  567.8 33.7 %reduce-scatter.8.cloned.1.call-done = f32[2,16,128]{2,1,0:T(8,128)} async-done(((f32[16,16,128]{2,1,0:T(8,128)}), f32[2,16,128]{2,1,0:T(8,128)}) %reduce-scatter.8.cloned.1.call-update) | async-done | bytes 16400 | tf_op jit(solution)/shard_map/reduce_scatter | solution.py:50
  601.5 0.8 multiply_reduce_fusion
  602.4 105.8 %psum.47 = f32[16]{0:T(128)S(1)} all-reduce(f32[16]{0:T(128)S(1)} %get-tuple-element.6), channel_id=1, replica_groups=mesh['dom'=64,'sub'=8] {'dom','sub'}, use_global_device_ids=true, to_apply=%region_14.15 | all-reduce | flops 16 | bytes 128 | tf_op jit(solution)/shard_map/psum | solution.py:54
  708.2 0.7 multiply_subtract_fusion
  (55 shorter events, 6.7 us)
Async XLA Ops:
  7.2 21.9 %copy-start = (f32[2,4,128,128]{3,2,1,0:T(8,128)S(1)}, f32[2,4,128,128]{3,2,1,0:T(8,128)}, u32[]{:S(2)}) copy-start(f32[2,4,128,128]{3,2,1,0:T(8,128)} %param.8) | copy-start | bytes 1572868
  7.2 68.2 %reduce-scatter.4.cloned.1.call-start = ((), (), s32[]{:S(2)}) async-start(), calls=%async_computation.3 | async-start | bytes 147456 | tf_op jit(solution)/shard_map/reduce_scatter | solution.py:50
  8.0 21.0 %copy-start.5 = (s32[2]{0:T(128)S(1)}, s32[2]{0:T(128)}, u32[]{:S(2)}) copy-start(s32[2]{0:T(128)} %param.10) | copy-start | bytes 28
  8.0 21.1 %copy-start.2 = (f32[2,16,128]{2,1,0:T(8,128)S(1)}, f32[2,16,128]{2,1,0:T(8,128)}, u32[]{:S(2)}) copy-start(f32[2,16,128]{2,1,0:T(8,128)} %param.6) | copy-start | bytes 49156
  27.6 1.5 copy-start.3
  27.6 7.0 collective-permute-start
  29.1 0.7 copy-start.4
  30.2 4.1 copy-start.1
  30.3 6.4 collective-permute-start.1
  37.4 301.1 %reduce-scatter.6.cloned.1.call-start = ((), (), s32[]{:S(2)}) async-start(), calls=%async_computation.4 | async-start | bytes 147456 | tf_op jit(solution)/shard_map/reduce_scatter | solution.py:50
  295.3 6.8 collective-permute-start.2
  297.1 6.4 collective-permute-start.3
  304.2 297.4 %reduce-scatter.8.cloned.1.call-start = ((), (), s32[]{:S(2)}) async-start(), calls=%async_computation.5 | async-start | bytes 147456 | tf_op jit(solution)/shard_map/reduce_scatter | solution.py:50
  558.2 6.8 collective-permute-start.4
  560.0 6.4 collective-permute-start.5
Sparse Core Ops, SparseCore 0:
  37.5 37.8 reduce-scatter.3
  304.3 34.2 reduce-scatter.5
  567.2 34.3 reduce-scatter.7
where the time goes:
time: 717 us; the launch traced here: 715 us
  blocking collectives  562 us (78%)
  waiting for transfers between devices  110 us (15%)
  starting transfers between devices  16.1 us (2%)
  between operations  14 us (2%)
    psum x3, blocking collectives, residual_sum(): return lax.psum(local_dots(residual_now, precond_now), ('dom', 'sub'))  304 us
    psum x2, blocking collectives, local(): curvature = lax.psum(local_dots(direction, image_vec), ('dom', 'sub'))  212 us
    reduce_scatter x3, waiting for transfers between devices, local(): lax.psum_scatter(spread[:group_rows] + incoming, 'sub', scatter_dimension...  104 us
    all_gather x3, blocking collectives, local(): own_group = lax.all_gather(direction, 'sub', axis=0, tiled=True)  46.1 us
    ppermute x6, starting transfers between devices, passed_along(): return lax.ppermute(x, axis, pairs)  16 us
  transfers between devices with their start and end apart: 9, of which 8 were waited for; matrix products, arithmetic and copies ran while one was open for 1% of the time, Pallas kernels for 0%

commit v1 on v0

--- a/solution.py
+++ b/solution.py
@@ -6,6 +6,14 @@
 K = 4
 ITERS = 3
 PRECISE = lax.Precision.HIGHEST
+
+
+def gather_by_exchange(shard, axis, dim):
+    size = lax.axis_size(axis)
+    repeats = [size if d == dim else 1 for d in range(shard.ndim)]
+    return lax.all_to_all(
+        jnp.tile(shard, repeats), axis, split_axis=dim, concat_axis=dim, tiled=True
+    )
 
 
 def passed_along(x, axis, by):
@@ -39,7 +47,7 @@
         own_part = jnp.einsum("rab,rzb->rza", upper_part, direction, precision=PRECISE)
         own_part = own_part + jnp.einsum("rba,rzb->rza", upper_part, direction, precision=PRECISE)
         own_part = own_part + cell_diagonal[:, None, :] * direction
-        own_group = lax.all_gather(direction, "sub", axis=0, tiled=True)
+        own_group = gather_by_exchange(direction, "sub", 0)
         next_group = passed_along(own_group, "dom", -1)
         window = jnp.concatenate([own_group, next_group], axis=0)
         far_rows = jnp.einsum("rkw,wzb->rkzb", picker, window, precision=PRECISE)

time: 717 us -> 689 us (0.961)
  blocking collectives: 562 us -> 516 us
  starting transfers between devices: 16.1 us -> 28.7 us
    all_gather x3 -> x0, blocking collectives: 46.1 us -> none  [local(): own_group = lax.all_gather(direction, 'sub', axis=0, tiled=True)]
    all_to_all x0 -> x3, starting transfers between devices: none -> 18.2 us  [gather_by_exchange(): lax.all_to_all(jnp.tile(shard, repeats), axis, split_axis=dim, concat_axi...]
    reduce_scatter x3, waiting for transfers between devices: 104 us -> 94.9 us  [local(): lax.psum_scatter(spread[:group_rows] + incoming, 'sub', scatter_dimension...]
  transfers between devices with their start and end apart: 9 -> 12, of which waited for: 8 -> 9; matrix products, arithmetic and copies ran while one was open for 1% -> 1% of each run, Pallas kernels for 0% -> 0%
where the time goes in v1:
time: 689 us; the launch traced here: 687 us
  blocking collectives  516 us (75%)
  waiting for transfers between devices  112 us (16%)
  starting transfers between devices  28.7 us (4%)
  between operations  14 us (2%)
    psum x3, blocking collectives, residual_sum(): return lax.psum(local_dots(residual_now, precond_now), ('dom', 'sub'))  305 us
    psum x2, blocking collectives, local(): curvature = lax.psum(local_dots(direction, image_vec), ('dom', 'sub'))  211 us
    reduce_scatter x3, waiting for transfers between devices, local(): lax.psum_scatter(spread[:group_rows] + incoming, 'sub', scatter_dimension...  94.9 us
    all_to_all x3, starting transfers between devices, gather_by_exchange(): lax.all_to_all(jnp.tile(shard, repeats), axis, split_axis=dim, concat_axi...  18.2 us
  transfers between devices with their start and end apart: 12, of which 9 were waited for; matrix products, arithmetic and copies ran while one was open for 1% of the time, Pallas kernels for 0%

profile of v1, /device:TPU:1, one launch (start us, length us, event | category | flops | bytes accessed | tf_op | source)
XLA Modules:
  0.0 687.1 jit_solution(1606716456555195304)
XLA Ops:
  7.2 0.8 broadcast_divide_fusion
  8.0 0.7 tile.12
  8.6 10.3 %all-to-all-start = ((f32[16,16,128]{2,1,0:T(8,128)}), f32[16,16,128]{2,1,0:T(8,128)S(1)}, u32[]{:S(2)}, u32[]{:S(2)}) async-start(f32[16,16,128]{2,1,0:T(8,128)} %bitcast.2), calls=%async_computation | async-start | bytes 262144 | tf_op jit(solution)/shard_map/all_to_all | solution.py:14
  20.8 1.3 collective-permute-start.1
  22.4 1.8 all-to-all-done
  24.2 1.3 collective-permute-start
  25.5 0.7 copy_add_fusion.2
  26.2 4.0 collective-permute-done
  31.3 35.4 %reduce-scatter.4.cloned.1.call-done = f32[2,16,128]{2,1,0:T(8,128)} async-done(((f32[16,16,128]{2,1,0:T(8,128)}), f32[2,16,128]{2,1,0:T(8,128)}) %reduce-scatter.4.cloned.1.call-update) | async-done | bytes 16400 | tf_op jit(solution)/shard_map/reduce_scatter | solution.py:58
  66.7 0.8 multiply_reduce_fusion.4
  67.5 105.8 %all-reduce = (f32[16]{0:T(128)S(1)}, f32[16]{0:T(128)S(1)}) all-reduce(f32[16]{0:T(128)S(1)} %get-tuple-element.3, f32[16]{0:T(128)S(1)} %get-tuple-element.2), channel_id=1, replica_groups=mesh['dom'=64,'sub'=8] {'dom','sub'}, use_global_device_ids=true, to_apply=%region_1.2 | all-reduce | flops 32 | bytes 256 | tf_op jit(solution)/shard_map/psum | solution.py:39
  173.4 99.4 %psum.44 = f32[16]{0:T(128)S(1)} all-reduce(f32[16]{0:T(128)S(1)} %get-tuple-element.12), channel_id=1, replica_groups=mesh['dom'=64,'sub'=8] {'dom','sub'}, use_global_device_ids=true, to_apply=%region_6.7 | all-reduce | flops 16 | bytes 128 | tf_op jit(solution)/shard_map/psum | solution.py:39
  273.9 3.9 all-to-all-start.1
  278.4 2.7 collective-permute-start.3
  281.4 1.8 all-to-all-done.1
  283.2 1.3 collective-permute-start.2
  284.5 0.7 copy_add_fusion.1
  285.2 4.0 collective-permute-done.2
  290.3 29.8 %reduce-scatter.6.cloned.1.call-done = f32[2,16,128]{2,1,0:T(8,128)} async-done(((f32[16,16,128]{2,1,0:T(8,128)}), f32[2,16,128]{2,1,0:T(8,128)}) %reduce-scatter.6.cloned.1.call-update) | async-done | bytes 16400 | tf_op jit(solution)/shard_map/reduce_scatter | solution.py:58
  320.0 0.8 multiply_reduce_fusion.2
  320.9 105.7 %psum.45 = f32[16]{0:T(128)S(1)} all-reduce(f32[16]{0:T(128)S(1)} %get-tuple-element.10), channel_id=1, replica_groups=mesh['dom'=64,'sub'=8] {'dom','sub'}, use_global_device_ids=true, to_apply=%region_9.10 | all-reduce | flops 16 | bytes 128 | tf_op jit(solution)/shard_map/psum | solution.py:62
  426.8 99.4 %psum.46 = f32[16]{0:T(128)S(1)} all-reduce(f32[16]{0:T(128)S(1)} %get-tuple-element.8), channel_id=1, replica_groups=mesh['dom'=64,'sub'=8] {'dom','sub'}, use_global_device_ids=true, to_apply=%region_11.12 | all-reduce | flops 16 | bytes 128 | tf_op jit(solution)/shard_map/psum | solution.py:39
  527.3 3.9 all-to-all-start.2
  531.7 2.7 collective-permute-start.5
  534.7 1.8 all-to-all-done.2
  536.5 1.3 collective-permute-start.4
  537.8 0.7 copy_add_fusion
  538.5 4.0 collective-permute-done.4
  543.6 29.8 %reduce-scatter.8.cloned.1.call-done = f32[2,16,128]{2,1,0:T(8,128)} async-done(((f32[16,16,128]{2,1,0:T(8,128)}), f32[2,16,128]{2,1,0:T(8,128)}) %reduce-scatter.8.cloned.1.call-update) | async-done | bytes 16400 | tf_op jit(solution)/shard_map/reduce_scatter | solution.py:58
  573.4 0.8 multiply_reduce_fusion
  574.2 105.7 %psum.47 = f32[16]{0:T(128)S(1)} all-reduce(f32[16]{0:T(128)S(1)} %get-tuple-element.6), channel_id=1, replica_groups=mesh['dom'=64,'sub'=8] {'dom','sub'}, use_global_device_ids=true, to_apply=%region_14.15 | all-reduce | flops 16 | bytes 128 | tf_op jit(solution)/shard_map/psum | solution.py:62
  679.9 0.7 multiply_subtract_fusion
  (61 shorter events, 9.5 us)
Async XLA Ops:
  7.2 11.8 %copy-start = (f32[2,4,128,128]{3,2,1,0:T(8,128)S(1)}, f32[2,4,128,128]{3,2,1,0:T(8,128)}, u32[]{:S(2)}) copy-start(f32[2,4,128,128]{3,2,1,0:T(8,128)} %param.8) | copy-start | bytes 1572868
  8.6 10.3 %copy-start.5 = (s32[2]{0:T(128)S(1)}, s32[2]{0:T(128)}, u32[]{:S(2)}) copy-start(s32[2]{0:T(128)} %param.10) | copy-start | bytes 28
  8.6 10.4 %copy-start.2 = (f32[2,16,128]{2,1,0:T(8,128)S(1)}, f32[2,16,128]{2,1,0:T(8,128)}, u32[]{:S(2)}) copy-start(f32[2,16,128]{2,1,0:T(8,128)} %param.6) | copy-start | bytes 49156
  8.6 15.6 %all-to-all-start = ((f32[16,16,128]{2,1,0:T(8,128)}), f32[16,16,128]{2,1,0:T(8,128)S(1)}, u32[]{:S(2)}, u32[]{:S(2)}) async-start(f32[16,16,128]{2,1,0:T(8,128)} %bitcast.2), calls=%async_computation | async-start | bytes 262144 | tf_op jit(solution)/shard_map/all_to_all | solution.py:14
  18.9 0.7 copy-start.3
  18.9 47.8 %reduce-scatter.4.cloned.1.call-start = ((), (), s32[]{:S(2)}) async-start(), calls=%async_computation.6 | async-start | bytes 147456 | tf_op jit(solution)/shard_map/reduce_scatter | solution.py:58
  19.6 0.7 copy-start.4
  20.7 1.4 copy-start.1
  20.8 4.7 collective-permute-start.1
  24.2 6.0 collective-permute-start
  273.9 9.2 %all-to-all-start.1 = ((f32[16,16,128]{2,1,0:T(8,128)}), f32[16,16,128]{2,1,0:T(8,128)S(1)}, u32[]{:S(2)}, u32[]{:S(2)}) async-start(f32[16,16,128]{2,1,0:T(8,128)} %bitcast.12), calls=%async_computation.2 | async-start | bytes 262144 | tf_op jit(solution)/shard_map/all_to_all | solution.py:14
  277.9 42.1 %reduce-scatter.6.cloned.1.call-start = ((), (), s32[]{:S(2)}) async-start(), calls=%async_computation.7 | async-start | bytes 147456 | tf_op jit(solution)/shard_map/reduce_scatter | solution.py:58
  278.4 6.1 collective-permute-start.3
  283.2 6.0 collective-permute-start.2
  527.3 9.2 %all-to-all-start.2 = ((f32[16,16,128]{2,1,0:T(8,128)}), f32[16,16,128]{2,1,0:T(8,128)S(1)}, u32[]{:S(2)}, u32[]{:S(2)}) async-start(f32[16,16,128]{2,1,0:T(8,128)} %bitcast.21), calls=%async_computation.4 | async-start | bytes 262144 | tf_op jit(solution)/shard_map/all_to_all | solution.py:14
  531.2 42.2 %reduce-scatter.8.cloned.1.call-start = ((), (), s32[]{:S(2)}) async-start(), calls=%async_computation.8 | async-start | bytes 147456 | tf_op jit(solution)/shard_map/reduce_scatter | solution.py:58
  531.7 6.1 collective-permute-start.5
  536.5 6.0 collective-permute-start.4
Sparse Core Ops, SparseCore 0:
  26.3 40.2 reduce-scatter.3
  285.3 34.6 reduce-scatter.5
  538.6 34.6 reduce-scatter.7
